TPU v7x, 512 devices: a whole 4x4x16 slice. The times are simulated.
512 devices in a mesh: param: 16 (over y, x_lo, core), example: 32 (over z, x_hi).
Axes of the slice: x: 4 (x_hi: 2, x_lo: 2; x = x_hi * 2 + x_lo), y: 4, z: 16, core: 2. Of those that a mesh axis runs over, the one named last changes fastest.
Arguments:
- train_grads: bfloat16 [24576, 32768], P('example', 'param'), may hold values from -6 to 6
- query_cache: bfloat16 [32, 256, 32768], P('example', None, 'param'), may hold values from -6 to 6
- left_inverse: float32 [32, 32, 32], replicated
- right_inverse: float32 [32, 32, 32], replicated
- module_of: int32 [32], replicated, may hold values from 0 to 31, each once
- owner: int32 [4], replicated, may hold values from 0 to 31, as said below
Outputs:
- scores: float32 [256, 4, 24576], P('param', None, 'example')
Inputs may be any that keep to these rules, and one draw needn't show every extreme that they name: A permutation: stored block j holds module module_of[j]. `owner`: the first and the last slot are each used in some turn.
All inputs are finite; a program needn't handle non-finite values.
Results may differ from a plain program's by a relative error of at most 0.0029.
Values may be sent and summed in bfloat16 or wider, within the bound.
A program may use at most 64 MiB of HBM per device.

v0:
```python
import math

import jax
import jax.numpy as jnp
from jax import lax
from jax.sharding import PartitionSpec as P


def spread(value, axis, source):
    kept = jnp.where(lax.axis_index(axis) == source, value, 0).astype(value.dtype)
    return lax.psum(kept, axis)


def body(train_grads, query_cache, left_inverse, right_inverse, module_of, owner):
    local_coords = train_grads.shape[1]
    size_in = left_inverse.shape[1]
    size_out = right_inverse.shape[1]
    local_mods = local_coords // (size_in * size_out)
    total_mods = module_of.shape[0]
    query_rows = query_cache.shape[1]
    slots_here = query_cache.shape[0]
    param_count = lax.axis_size("param")
    factor = 1.0 / math.sqrt(local_coords * param_count)
    param_index = lax.axis_index("param")
    local_ids = lax.dynamic_slice_in_dim(module_of, param_index * local_mods, local_mods)
    selector = (local_ids[:, None] == jnp.arange(total_mods, dtype=jnp.int32)[None, :]).astype(
        jnp.float32
    )
    left_local = jnp.einsum("jm,mab->jab", selector, left_inverse, precision=lax.Precision.HIGHEST)
    right_local = jnp.einsum(
        "jm,mab->jab", selector, right_inverse, precision=lax.Precision.HIGHEST
    )
    collected = []
    for turn in range(owner.shape[0]):
        slot = owner[turn]
        root_index = slot // slots_here
        raw = lax.dynamic_index_in_dim(query_cache, slot % slots_here, 0, keepdims=False)
        blocks = raw.astype(jnp.float32).reshape(query_rows, local_mods, size_in, size_out)
        mixed = jnp.einsum(
            "mab,qmbc,mcd->qmad", left_local, blocks, right_local, precision=lax.Precision.HIGHEST
        )
        whitened = spread(
            (mixed * factor).reshape(query_rows, local_coords).astype(jnp.bfloat16),
            "example",
            root_index,
        )
        collected.append(
            lax.psum_scatter(
                lax.dot_general(
                    whitened,
                    train_grads,
                    (((1,), (1,)), ((), ())),
                    preferred_element_type=jnp.float32,
                ),
                "param",
                scatter_dimension=0,
                tiled=True,
            )
        )
    scores = jnp.stack(collected, axis=1)
    return scores


def solution(mesh):
    placed = (P("example", "param"), P("example", None, "param"), P(), P(), P(), P())
    return jax.shard_map(
        body, mesh=mesh, in_specs=placed, out_specs=P("param", None, "example"), check_vma=False
    )
```

profile of v0, /device:TPU:1, one launch (start us, length us, event | category | flops | bytes accessed | tf_op | source)
XLA Modules:
  0.0 641.8 jit_solution(13111378020737200701)
XLA Ops:
  6.5 0.0 copy-start
  6.5 0.0 all-reduce.3.cloned.1.call-start
  6.5 1.5 fusion.15
  10.5 0.7 dynamic_slice.8
  11.3 1.6 convolution_bitcast_fusion.1
  12.9 1.6 convolution_bitcast_fusion
  14.5 2.3 copy.8
  16.7 2.5 fusion.5
  19.2 5.7 broadcast_select_fusion.3
  24.9 0.0 all-reduce.3.cloned.1.call-update
  24.9 0.0 reduce-scatter.11.cloned.1.call-start
  25.0 313.7 %all-reduce.3.cloned.1.call-done = (bf16[256,2048]{0,1:T(8,128)(2,1)}, bf16[256,2048]{0,1:T(8,128)(2,1)}, bf16[256,2048]{0,1:T(8,128)(2,1)}, bf16[256,2048]{0,1:T(8,128)(2,1)}) async-done(((bf16[256,2048]{0,1:T(8,128)(2,1)}, bf16[256,2048]{0,1:T(8,128)(2,1)}, bf16[256,2048]{0,1:T(8,128)(2,1)}, bf16[256,2048]{0,1:T(8,128)(2,1)}), (bf16[256,2048]{0,1:T(8,128)(2,1)}, bf16[256,2048]{0,1:T(8,128)(2,1)}, ...) | async-done | bytes 4194320 | tf_op jit(solution)/shard_map/psum | solution.py:11
  338.7 0.0 copy-done
  338.7 3.1 fusion.19
  341.8 0.0 reduce-scatter.11.cloned.1.call-update
  341.8 0.0 reduce-scatter.9.cloned.1.call-start
  341.9 3.1 fusion.18
  345.0 0.0 reduce-scatter.9.cloned.1.call-update
  345.0 0.0 reduce-scatter.5.cloned.1.call-start
  345.1 3.1 fusion.16
  348.2 0.0 reduce-scatter.5.cloned.1.call-update
  348.2 0.0 reduce-scatter.7.cloned.1.call-start
  348.3 3.2 fusion.17
  351.5 0.0 reduce-scatter.7.cloned.1.call-update
  351.5 71.3 %reduce-scatter.11.cloned.1.call-done = f32[16,768]{1,0:T(8,128)} async-done(((f32[256,768]{1,0:T(8,128)}), f32[16,768]{1,0:T(8,128)}) %reduce-scatter.11.cloned.1.call-update) | async-done | bytes 49168 | tf_op jit(solution)/shard_map/reduce_scatter | solution.py:48
  422.7 70.5 %reduce-scatter.9.cloned.1.call-done = f32[16,768]{1,0:T(8,128)} async-done(((f32[256,768]{1,0:T(8,128)}), f32[16,768]{1,0:T(8,128)}) %reduce-scatter.9.cloned.1.call-update) | async-done | bytes 49168 | tf_op jit(solution)/shard_map/reduce_scatter | solution.py:48
  493.2 70.1 %reduce-scatter.5.cloned.1.call-done = f32[16,768]{1,0:T(8,128)} async-done(((f32[256,768]{1,0:T(8,128)}), f32[16,768]{1,0:T(8,128)}) %reduce-scatter.5.cloned.1.call-update) | async-done | bytes 49168 | tf_op jit(solution)/shard_map/reduce_scatter | solution.py:48
  563.3 70.3 %reduce-scatter.7.cloned.1.call-done = f32[16,768]{1,0:T(8,128)} async-done(((f32[256,768]{1,0:T(8,128)}), f32[16,768]{1,0:T(8,128)}) %reduce-scatter.7.cloned.1.call-update) | async-done | bytes 49168 | tf_op jit(solution)/shard_map/reduce_scatter | solution.py:48
  633.6 0.9 pad_maximum_fusion
  634.5 0.8 copy.9
Async XLA Ops:
  6.5 332.1 %copy-start = (bf16[768,2048]{1,0:T(8,128)(2,1)S(1)}, bf16[768,2048]{1,0:T(8,128)(2,1)}, u32[]{:S(2)}) copy-start(bf16[768,2048]{1,0:T(8,128)(2,1)} %param.6) | copy-start | bytes 9437188
  6.5 332.1 %all-reduce.3.cloned.1.call-start = ((), (), s32[]{:S(2)}) async-start(), calls=%async_computation.8 | async-start | bytes 8388608 | tf_op jit(solution)/shard_map/psum | solution.py:11
  24.9 397.8 %reduce-scatter.11.cloned.1.call-start = ((), (), s32[]{:S(2)}) async-start(), calls=%async_computation.7 | async-start | bytes 835584 | tf_op jit(solution)/shard_map/reduce_scatter | solution.py:48
  341.8 151.4 %reduce-scatter.9.cloned.1.call-start = ((), (), s32[]{:S(2)}) async-start(), calls=%async_computation.6 | async-start | bytes 835584 | tf_op jit(solution)/shard_map/reduce_scatter | solution.py:48
  345.0 218.3 %reduce-scatter.5.cloned.1.call-start = ((), (), s32[]{:S(2)}) async-start(), calls=%async_computation.4 | async-start | bytes 835584 | tf_op jit(solution)/shard_map/reduce_scatter | solution.py:48
  348.2 285.3 %reduce-scatter.7.cloned.1.call-start = ((), (), s32[]{:S(2)}) async-start(), calls=%async_computation.5 | async-start | bytes 835584 | tf_op jit(solution)/shard_map/reduce_scatter | solution.py:48
Sparse Core Ops, SparseCore 0:
  25.1 313.5 all-reduce.2
  342.0 80.7 reduce-scatter.10
  425.8 67.3 reduce-scatter.8
  495.9 67.3 reduce-scatter.4
  566.2 67.3 reduce-scatter.6
where the time goes:
time: 644 us; the launch traced here: 642 us
  waiting for transfers between devices  596 us (93%)
  matrix products  23.9 us (4%)
  between operations  15.6 us (2%)
    psum x1, waiting for transfers between devices, spread(): return lax.psum(kept, axis)  314 us
    reduce_scatter x4, waiting for transfers between devices, body(): lax.psum_scatter(lax.dot_general(whitened, train_grads, (((1,), (1,)), ((...  282 us
  transfers between devices with their start and end apart: 5, of which 5 were waited for; matrix products, arithmetic and copies ran while one was open for 1% of the time, Pallas kernels for 0%

commit v1 on v0

v1 whole, which is shorter than its diff:
```python
import functools
import math

import jax
import jax.numpy as jnp
from jax import lax
from jax.experimental import pallas as pl
from jax.experimental.pallas import tpu as pltpu
from jax.sharding import PartitionSpec as P

LANES = 256
DELAY = 3
MESH = pl.DeviceIdType.MESH


def kernel(
    cfg,
    train_hbm,
    query_hbm,
    left_ref,
    right_ref,
    module_ref,
    owner_ref,
    out_ref,
    query,
    train,
    spread_left,
    spread_right,
    kron_high,
    kron_low,
    mine,
    other,
    landed,
    passed,
    total,
    kept,
    outgoing,
    incoming,
    load_sem,
    swap_send,
    swap_recv,
    ring_send,
    ring_recv,
    sum_send,
    sum_recv,
):
    groups, ring, turns, rows, coords, steps, half, lanes, delay = cfg
    pieces = coords // lanes
    blocks = coords // 1024
    param = lax.axis_index("param")
    example = lax.axis_index("example")
    plane = lax.div(example, 2)
    side = lax.rem(example, 2)
    partner = plane * 2 + 1 - side
    following = lax.rem(plane + 1, ring) * 2 + side
    previous = lax.rem(plane + ring - 1, ring) * 2 + side
    lag = (ring - 1) * delay
    sent = steps - delay

    barrier = pltpu.get_barrier_semaphore()
    for place in (partner, following, previous):
        pl.semaphore_signal(
            barrier, inc=1, device_id={"example": place}, device_id_type=MESH
        )

    @pl.loop(1, groups)
    def _(hop):
        pl.semaphore_signal(
            barrier,
            inc=1,
            device_id={"param": lax.rem(param + hop, groups)},
            device_id_type=MESH,
        )

    load_query = pltpu.make_async_copy(query_hbm.at[0], query, load_sem.at[0])
    load_query.start()
    load_train = [
        pltpu.make_async_copy(
            train_hbm.at[:, pl.ds(k * lanes, lanes)], train.at[k], load_sem.at[1 + k]
        )
        for k in range(pieces)
    ]
    for copy in load_train:
        copy.start()

    factor = 1.0 / math.sqrt(coords * groups)
    col = lax.broadcasted_iota(jnp.int32, (32, 1024), 1)
    row = lax.broadcasted_iota(jnp.int32, (32, 1024), 0)
    pick_outer = (lax.shift_right_logical(col, 5) == row).astype(jnp.float32)
    pick_inner = (lax.bitwise_and(col, 31) == row).astype(jnp.float32)
    load_query.wait()
    for block in range(blocks):
        module = module_ref[param * blocks + block]
        spread_left[...] = lax.dot_general(
            left_ref[module] * factor,
            pick_outer,
            (((0,), (0,)), ((), ())),
            precision=lax.Precision.HIGHEST,
            preferred_element_type=jnp.float32,
        )
        spread_right[...] = lax.dot_general(
            right_ref[module],
            pick_inner,
            (((1,), (0,)), ((), ())),
            precision=lax.Precision.HIGHEST,
            preferred_element_type=jnp.float32,
        )

        @pl.loop(0, 32)
        def _(b):
            product = spread_left[pl.ds(b, 1), :] * spread_right[...]
            high = product.astype(jnp.bfloat16)
            low = (product - high.astype(jnp.float32)).astype(jnp.bfloat16)
            at = pl.ds(pl.multiple_of(b * 32, 32), 32)
            kron_high[at, :] = high
            kron_low[at, :] = low

        source = query[:, block * 1024 : (block + 1) * 1024]
        for k in range(1024 // lanes):
            cut = slice(k * lanes, (k + 1) * lanes)
            mixed = jnp.dot(
                source, kron_high[:, cut], preferred_element_type=jnp.float32
            ) + jnp.dot(source, kron_low[:, cut], preferred_element_type=jnp.float32)
            mine[:, block * (1024 // lanes) + k] = mixed.astype(jnp.bfloat16).reshape(
                groups, 16, lanes
            )

    pl.semaphore_wait(barrier, groups + 2)

    def place_of(order):
        return lax.rem(order + param, groups)

    def swap(order):
        at = place_of(order)
        return pltpu.make_async_remote_copy(
            src_ref=mine.at[at],
            dst_ref=other.at[at],
            send_sem=swap_send.at[order],
            recv_sem=swap_recv.at[order],
            device_id={"example": partner},
            device_id_type=MESH,
        )

    @pl.loop(0, groups // 2)
    def _(j):
        swap(j).start()
        swap(groups - 1 - j).start()

    roots = [lax.div(owner_ref[t], 2) for t in range(turns)]
    sides = [lax.rem(owner_ref[t], 2) for t in range(turns)]
    ahead = [lax.rem(plane - r + ring, ring) for r in roots]
    behind = [lax.rem(r - plane + ring, ring) for r in roots]

    def ring_copy(way, s):
        at = way * steps + s
        land = way * sent + s
        return pltpu.make_async_remote_copy(
            src_ref=passed.at[at],
            dst_ref=landed.at[land],
            send_sem=ring_send.at[land],
            recv_sem=ring_recv.at[land],
            device_id={"example": following if way == 0 else previous},
            device_id_type=MESH,
        )

    def advance(s, first, last):
        j = lax.div(s, pieces)
        k = lax.rem(s, pieces)

        @pl.when(jnp.logical_and(k == 0, j < groups // 2))
        def _():
            swap(j).wait_recv()
            swap(groups - 1 - j).wait_recv()

        for way in range(2):
            order = j if way == 0 else groups - 1 - j
            piece = k if way == 0 else pieces - 1 - k
            here = mine[place_of(order), piece]
            there = other[place_of(order), piece]
            if not first:
                ring_copy(way, s - delay).wait_recv()
            for t in range(turns):
                value = jnp.where(sides[t] == side, here, there)
                if not first:
                    value = jnp.where(
                        ahead[t] == 0, value, landed[way * sent + s - delay, t]
                    )
                passed[way * steps + s, t] = value
            if not last:
                ring_copy(way, s).start()

    def sum_copy(order):
        return pltpu.make_async_remote_copy(
            src_ref=outgoing.at[order],
            dst_ref=incoming.at[order],
            send_sem=sum_send.at[order],
            recv_sem=sum_recv.at[order],
            device_id={"param": place_of(order)},
            device_id_type=MESH,
        )

    def compute(i):
        j = lax.div(i, pieces)
        k = lax.rem(i, pieces)
        for way in range(2):
            near, far = (ahead, behind) if way == 0 else (behind, ahead)
            parts = []
            for t in range(turns):
                direct = i + delay * near[t]
                around = (2 * half - 1 - i) + delay * far[t]
                at = jnp.where(
                    direct < steps, way * steps + direct, (1 - way) * steps + around
                )
                parts.append(passed[at, t])
            left = jnp.concatenate(parts, axis=0)
            piece = k if way == 0 else pieces - 1 - k
            product = lax.dot_general(
                left,
                train[piece],
                (((1,), (1,)), ((), ())),
                preferred_element_type=jnp.float32,
            )

            @pl.when(k == 0)
            def _():
                total[way] = product

            @pl.when(k > 0)
            def _():
                total[way] += product

        @pl.when(k == pieces - 1)
        def _():
            @pl.when(j == 0)
            def _():
                kept[...] = total[0]

            @pl.when(j > 0)
            def _():
                outgoing[j] = total[0].astype(jnp.bfloat16)
                sum_copy(j).start()

            outgoing[groups - 1 - j] = total[1].astype(jnp.bfloat16)
            sum_copy(groups - 1 - j).start()

    @pl.loop(0, delay)
    def _(s):
        advance(s, True, False)

    @pl.loop(delay, lag)
    def _(s):
        advance(s, False, False)

    for copy in load_train:
        copy.wait()

    @pl.loop(lag, sent)
    def _(s):
        advance(s, False, False)
        compute(s - lag)

    @pl.loop(sent, steps)
    def _(s):
        advance(s, False, True)
        compute(s - lag)

    @pl.loop(steps - lag, half)
    def _(i):
        compute(i)

    @pl.loop(0, sent)
    def _(s):
        ring_copy(0, s).wait_send()
        ring_copy(1, s).wait_send()

    @pl.loop(0, groups)
    def _(order):
        swap(order).wait_send()

    @pl.loop(1, groups)
    def _(order):
        sum_copy(order).wait()
        kept[...] += incoming[order].astype(jnp.float32)

    for t in range(turns):
        out_ref[:, t, :] = kept[t * 16 : (t + 1) * 16, :]


def body(train_grads, query_cache, left_inverse, right_inverse, module_of, owner):
    groups = lax.axis_size("param")
    ring = lax.axis_size("example") // 2
    turns = owner.shape[0]
    rows, coords = train_grads.shape
    queries = query_cache.shape[1]
    lanes, delay = LANES, DELAY
    pieces = coords // lanes
    half = groups * pieces // 2
    steps = half + ring // 2 * delay
    sent = steps - delay
    cfg = (groups, ring, turns, rows, coords, steps, half, lanes, delay)
    bf16, f32 = jnp.bfloat16, jnp.float32
    dma = pltpu.SemaphoreType.DMA
    return pl.pallas_call(
        functools.partial(kernel, cfg),
        out_shape=jax.ShapeDtypeStruct((queries // groups, turns, rows), f32),
        in_specs=[
            pl.BlockSpec(memory_space=pl.ANY),
            pl.BlockSpec(memory_space=pl.ANY),
            pl.BlockSpec(memory_space=pltpu.VMEM),
            pl.BlockSpec(memory_space=pltpu.VMEM),
            pl.BlockSpec(memory_space=pltpu.SMEM),
            pl.BlockSpec(memory_space=pltpu.SMEM),
        ],
        out_specs=pl.BlockSpec(memory_space=pltpu.VMEM),
        scratch_shapes=[
            pltpu.VMEM((queries, coords), bf16),
            pltpu.VMEM((pieces, rows, lanes), bf16),
            pltpu.VMEM((32, 1024), f32),
            pltpu.VMEM((32, 1024), f32),
            pltpu.VMEM((1024, 1024), bf16),
            pltpu.VMEM((1024, 1024), bf16),
            pltpu.VMEM((groups, pieces, 16, lanes), bf16),
            pltpu.VMEM((groups, pieces, 16, lanes), bf16),
            pltpu.VMEM((2 * sent, turns, 16, lanes), bf16),
            pltpu.VMEM((2 * steps, turns, 16, lanes), bf16),
            pltpu.VMEM((2, 16 * turns, rows), f32),
            pltpu.VMEM((16 * turns, rows), f32),
            pltpu.VMEM((groups, 16 * turns, rows), bf16),
            pltpu.VMEM((groups, 16 * turns, rows), bf16),
            dma((1 + pieces,)),
            dma((groups,)),
            dma((groups,)),
            dma((2 * sent,)),
            dma((2 * sent,)),
            dma((groups,)),
            dma((groups,)),
        ],
        compiler_params=pltpu.CompilerParams(
            collective_id=0, has_side_effects=True, vmem_limit_bytes=56 * 1024 * 1024
        ),
    )(train_grads, query_cache, left_inverse, right_inverse, module_of, owner)


def solution(mesh):
    placed = (P("example", "param"), P("example", None, "param"), P(), P(), P(), P())
    return jax.shard_map(
        body, mesh=mesh, in_specs=placed, out_specs=P("param", None, "example"), check_vma=False
    )
```

time: 644 us -> 145 us (0.23)
  waiting for transfers between devices: 596 us -> 0 us
  Pallas kernels: 0 us -> 144 us
  matrix products: 23.9 us -> 0 us
  between operations: 15.6 us -> 0.01 us
    psum x1 -> x0, waiting for transfers between devices: 314 us -> none  [spread(): return lax.psum(kept, axis)]
    reduce_scatter x4 -> x0, waiting for transfers between devices: 282 us -> none  [body(): lax.psum_scatter(lax.dot_general(whitened, train_grads, (((1,), (1,)), ((...]
    pallas_call x0 -> x1, Pallas kernels: none -> 144 us  [body(): pl.pallas_call(functools.partial(kernel, cfg), out_shape=jax.ShapeDtypeSt...]
    dot_general x8 -> x0, matrix products: 23.9 us -> none  [the longest x4 12.6 us: body(): lax.dot_general(whitened, train_grads, (((1,), (1,)), ((), ())), preferre...]
  transfers between devices with their start and end apart: 5 -> 0, of which waited for: 5 -> 0; matrix products, arithmetic and copies ran while one was open for 1% -> 0% of each run, Pallas kernels for 0% -> 0%
where the time goes in v1:
time: 145 us
  Pallas kernels  144 us (99%)
  local copies, waits for them, and re-layouts  1.62 us (1%)
    pallas_call x1, Pallas kernels, body(): pl.pallas_call(functools.partial(kernel, cfg), out_shape=jax.ShapeDtypeSt...  144 us

profile of v1, /device:TPU:1, one launch (start us, length us, event | category | flops | bytes accessed | tf_op | source)
XLA Modules:
  0.0 145.1 jit_solution(3449285473492302203)
XLA Ops:
  0.0 143.5 %shard_map.64 = f32[16,4,768]{2,1,0:T(4,128)} custom-call(bf16[768,2048]{1,0:T(8,128)(2,1)} %train_hbm.1, bf16[1,256,2048]{2,1,0:T(8,128)(2,1)} %query_hbm.1, f32[32,32,32]{2,1,0:T(8,128)} %left_ref.1, f32[32,32,32]{2,1,0:T(8,128)} %right_ref.1, s32[32]{0:T(128)} %module_ref.1, s32[4]{0:T(128)} %owner_ref.1), custom_call_target="tpu_custom_call" | custom-call | tf_op jit(solution)/shard_map/pallas_call | solution.py:303
  143.5 1.6 %copy.8 = f32[16,4,768]{2,1,0:T(4,128)} copy(f32[16,4,768]{2,1,0:T(4,128)} %shard_map.64) | data formatting | bytes 393216

commit v2 on v1

v2 whole, which is shorter than its diff:
```python
import functools
import math

import jax
import jax.numpy as jnp
from jax import lax
from jax.experimental import pallas as pl
from jax.experimental.pallas import tpu as pltpu
from jax.sharding import PartitionSpec as P

LANES = 256
PIECES = 4
BLOCK = LANES * PIECES
GROUPS = 16
BATCH = 4
TILE = 256
PARCEL = 128
MESH = pl.DeviceIdType.MESH
BF16, F32 = jnp.bfloat16, jnp.float32
ACROSS = (((1,), (1,)), ((), ()))


def kernel(
    ring,
    turns,
    train_hbm,
    query_hbm,
    left_ref,
    right_ref,
    module_ref,
    owner_ref,
    out_ref,
    query,
    train,
    spread_left,
    spread_right,
    kron_high,
    kron_low,
    swapper,
    mine,
    other,
    landed,
    passed,
    gathered,
    sorted_rows,
    product,
    summed,
    crossed,
    ordered,
    outgoing,
    incoming,
    load_sem,
    swap_send,
    swap_recv,
    train_send,
    train_recv,
    ring_send,
    ring_recv,
    sum_send,
    sum_recv,
    cross_send,
    cross_recv,
):
    owners = lax.axis_size("param")
    param = lax.axis_index("param")
    example = lax.axis_index("example")
    plane = lax.div(example, 2)
    side = lax.rem(example, 2)
    partner = plane * 2 + 1 - side
    following = lax.rem(plane + 1, ring) * 2 + side
    previous = lax.rem(plane + ring - 1, ring) * 2 + side
    reach = ring // 2
    laps = GROUPS // 2 + reach
    steps = laps * PIECES
    sent = steps - PIECES
    batches = GROUPS // BATCH
    own_tiles = train_hbm.shape[0] // TILE
    tiles = 2 * own_tiles

    barrier = pltpu.get_barrier_semaphore()
    for place in (partner, following, previous):
        pl.semaphore_signal(
            barrier, inc=1, device_id={"example": place}, device_id_type=MESH
        )

    @pl.loop(1, owners)
    def _(hop):
        pl.semaphore_signal(
            barrier,
            inc=1,
            device_id={"param": lax.rem(param + hop, owners)},
            device_id_type=MESH,
        )

    load_query = pltpu.make_async_copy(query_hbm.at[0], query, load_sem.at[0])
    load_query.start()
    here_lanes = pl.ds(pl.multiple_of(side * BLOCK, BLOCK), BLOCK)
    there_lanes = pl.ds(pl.multiple_of((1 - side) * BLOCK, BLOCK), BLOCK)
    load_train = [
        pltpu.make_async_copy(
            train_hbm.at[pl.ds(j * TILE, TILE), here_lanes], train.at[j], load_sem.at[1 + j]
        )
        for j in range(own_tiles)
    ]
    for copy in load_train:
        copy.start()
    parcels = own_tiles * (TILE // PARCEL)

    def give_train(i):
        return pltpu.make_async_remote_copy(
            src_ref=train_hbm.at[pl.ds(pl.multiple_of(i * PARCEL, PARCEL), PARCEL), there_lanes],
            dst_ref=train.at[
                own_tiles + lax.div(i, TILE // PARCEL),
                pl.ds(pl.multiple_of(lax.rem(i, TILE // PARCEL) * PARCEL, PARCEL), PARCEL),
            ],
            send_sem=train_send.at[i],
            recv_sem=train_recv.at[i],
            device_id={"example": partner},
            device_id_type=MESH,
        )

    row = lax.broadcasted_iota(jnp.int32, (256, 256), 0)
    col = lax.broadcasted_iota(jnp.int32, (256, 256), 1)
    swapper[...] = (lax.bitwise_and(col, 15) * 16 + lax.shift_right_logical(col, 4) == row).astype(
        F32
    ).astype(BF16)

    factor = 1.0 / math.sqrt(2 * BLOCK * owners)
    col = lax.broadcasted_iota(jnp.int32, (32, BLOCK), 1)
    row = lax.broadcasted_iota(jnp.int32, (32, BLOCK), 0)
    pick_outer = (lax.shift_right_logical(col, 5) == row).astype(F32)
    pick_inner = (lax.bitwise_and(col, 31) == row).astype(F32)
    for block in range(2):
        module = module_ref[param * 2 + block]
        spread_left[...] = lax.dot_general(
            left_ref[module] * factor,
            pick_outer,
            (((0,), (0,)), ((), ())),
            precision=lax.Precision.HIGHEST,
            preferred_element_type=F32,
        )
        spread_right[...] = lax.dot_general(
            right_ref[module],
            pick_inner,
            (((1,), (0,)), ((), ())),
            precision=lax.Precision.HIGHEST,
            preferred_element_type=F32,
        )

        @pl.loop(0, 32)
        def _(b):
            exact = spread_left[pl.ds(b, 1), :] * spread_right[...]
            high = exact.astype(BF16)
            low = (exact - high.astype(F32)).astype(BF16)
            at = pl.ds(pl.multiple_of(b * 32, 32), 32)
            kron_high[at, :] = high
            kron_low[at, :] = low

        if block == 0:
            pl.semaphore_wait(barrier, owners + 2)
            give_train(0).start()
            load_query.wait()
        source = jnp.dot(
            swapper[...], query[:, block * BLOCK : (block + 1) * BLOCK], preferred_element_type=F32
        ).astype(BF16)
        for k in range(BLOCK // TILE):
            cut = slice(k * TILE, (k + 1) * TILE)
            mixed = jnp.dot(source, kron_high[:, cut], preferred_element_type=F32) + jnp.dot(
                source, kron_low[:, cut], preferred_element_type=F32
            )
            mixed = mixed.astype(BF16)
            for part in range(TILE // LANES):
                mine[block, :, k * (TILE // LANES) + part] = mixed[
                    :, part * LANES : (part + 1) * LANES
                ].reshape(GROUPS, 16, LANES)

    def swap(order):
        return pltpu.make_async_remote_copy(
            src_ref=mine.at[1 - side, order],
            dst_ref=other.at[order],
            send_sem=swap_send.at[order],
            recv_sem=swap_recv.at[order],
            device_id={"example": partner},
            device_id_type=MESH,
        )

    @pl.loop(0, GROUPS // 2)
    def _(j):
        swap(j).start()
        swap(GROUPS - 1 - j).start()

    @pl.loop(1, parcels)
    def _(i):
        give_train(i).start()

    roots = [lax.div(owner_ref[t], 2) for t in range(turns)]
    sides = [lax.rem(owner_ref[t], 2) for t in range(turns)]
    ahead = [lax.rem(plane - r + ring, ring) for r in roots]
    near = [jnp.where(a <= reach, 0, 1) for a in ahead]
    far_off = [jnp.where(a <= reach, a, ring - a) for a in ahead]
    spare = [reach - f for f in far_off]

    def ring_copy(way, s):
        return pltpu.make_async_remote_copy(
            src_ref=passed.at[way * steps + s],
            dst_ref=landed.at[way * sent + s],
            send_sem=ring_send.at[way * sent + s],
            recv_sem=ring_recv.at[way * sent + s],
            device_id={"example": following if way == 0 else previous},
            device_id_type=MESH,
        )

    def advance(s, first, last):
        j = lax.div(s, PIECES)
        k = lax.rem(s, PIECES)

        @pl.when(jnp.logical_and(k == 0, j < GROUPS // 2))
        def _():
            swap(j).wait_recv()
            swap(GROUPS - 1 - j).wait_recv()

        for way in range(2):
            order = j if way == 0 else GROUPS - 1 - j
            here = mine[side, order, k]
            there = other[order, k]
            if not first:
                ring_copy(way, s - PIECES).wait_recv()
            for t in range(turns):
                value = jnp.where(sides[t] == side, here, there)
                if not first:
                    value = jnp.where(
                        ahead[t] == 0, value, landed[way * sent + s - PIECES, t]
                    )
                passed[way * steps + s, t] = value
            if not last:
                ring_copy(way, s).start()

    def gather(b):
        for u in range(BATCH):
            v = BATCH * b + u
            w = (BATCH // 2) * b + u // 2
            for t in range(turns):
                early = v < 2 * spare[t]
                if u % 2 == 0:
                    way = near[t]
                    lap = jnp.where(early, v, spare[t] + w) + far_off[t]
                else:
                    way = jnp.where(early, near[t], 1 - near[t])
                    lap = jnp.where(early, v + far_off[t], w - spare[t] + ring - far_off[t])
                base = way * steps + lap * PIECES
                for k in range(PIECES):
                    gathered[
                        (u * turns + t) * 16 : (u * turns + t + 1) * 16,
                        k * LANES : (k + 1) * LANES,
                    ] = passed[base + k, t]
        sorted_rows[...] = jnp.dot(
            swapper[...], gathered[...], preferred_element_type=F32
        ).astype(BF16)

    def multiply(b, j):
        product[...] = lax.dot_general(
            sorted_rows[...], train[j], ACROSS, preferred_element_type=F32
        )
        outgoing[b, :, j] = product[...].astype(BF16).reshape(owners, 16, TILE)
        summed[b, j] = product[pl.ds(pl.multiple_of(param * 16, 16), 16), :]

    def sum_copy(b, hop):
        return pltpu.make_async_remote_copy(
            src_ref=outgoing.at[b, lax.rem(param + hop, owners)],
            dst_ref=incoming.at[b, hop],
            send_sem=sum_send.at[b, hop],
            recv_sem=sum_recv.at[b, hop],
            device_id={"param": lax.rem(param + hop, owners)},
            device_id_type=MESH,
        )

    def give(b):
        @pl.loop(1, owners)
        def _(hop):
            sum_copy(b, hop).start()

    def cross(b):
        return pltpu.make_async_remote_copy(
            src_ref=summed.at[b, pl.ds(own_tiles, own_tiles)],
            dst_ref=crossed.at[b],
            send_sem=cross_send.at[b],
            recv_sem=cross_recv.at[b],
            device_id={"example": partner},
            device_id_type=MESH,
        )

    def finish(b):
        @pl.loop(1, owners)
        def _(hop):
            sum_copy(b, hop).wait_recv()
            summed[b] += incoming[b, hop].astype(F32)

        cross(b).start()

    start = (reach + 2) * PIECES

    @pl.loop(0, PIECES)
    def _(s):
        advance(s, True, False)

    @pl.loop(PIECES, start)
    def _(s):
        advance(s, False, False)

    for copy in load_train:
        copy.wait()

    @pl.loop(start, sent)
    def _(s):
        advance(s, False, False)
        lap = lax.div(s - start, PIECES)
        k = lax.rem(s, PIECES)
        b = lax.div(lap, 2)
        turn_of_batch = lax.rem(lap, 2) == 0

        @pl.when(jnp.logical_and(turn_of_batch, k == 0))
        def _():
            gather(b)

        @pl.when(jnp.logical_and(turn_of_batch, k == 1))
        def _():
            @pl.loop(0, own_tiles)
            def _(j):
                multiply(b, j)

        @pl.when(jnp.logical_and(turn_of_batch, k == 2))
        def _():
            @pl.when(b == 0)
            def _():
                @pl.loop(0, parcels)
                def _(i):
                    give_train(i).wait_recv()

            @pl.loop(own_tiles, tiles)
            def _(j):
                multiply(b, j)

        @pl.when(jnp.logical_and(turn_of_batch, k == PIECES - 1))
        def _():
            give(b)

    @pl.loop(sent, steps)
    def _(s):
        advance(s, False, True)

    gather(batches - 1)

    @pl.loop(0, tiles)
    def _(j):
        multiply(batches - 1, j)

    give(batches - 1)

    @pl.loop(0, batches)
    def _(b):
        finish(b)

    @pl.loop(0, sent)
    def _(s):
        ring_copy(0, s).wait_send()
        ring_copy(1, s).wait_send()

    @pl.loop(0, GROUPS)
    def _(order):
        swap(order).wait_send()

    @pl.loop(0, parcels)
    def _(i):
        give_train(i).wait_send()

    @pl.loop(0, batches)
    def _(b):
        @pl.loop(1, owners)
        def _(hop):
            sum_copy(b, hop).wait_send()

    for b in range(batches):
        cross(b).wait()
        for j in range(own_tiles):
            ordered[j, b * 16 : (b + 1) * 16, :] = summed[b, j] + crossed[b, j]

    for t in range(turns):

        @pl.loop(0, GROUPS)
        def _(i):
            a = jnp.where(near[t] == 0, i, GROUPS - 1 - i)
            v = jnp.where(
                a < 2 * spare[t],
                a,
                jnp.where(
                    a < GROUPS // 2 + spare[t],
                    2 * (a - spare[t]),
                    2 * (GROUPS - 1 - a + spare[t]) + 1,
                ),
            )
            for j in range(own_tiles):
                out_ref[i, t : t + 1, j * TILE : (j + 1) * TILE] = ordered[
                    j, pl.ds(v * turns + t, 1), :
                ]


def body(train_grads, query_cache, left_inverse, right_inverse, module_of, owner):
    owners = lax.axis_size("param")
    ring = lax.axis_size("example") // 2
    turns = owner.shape[0]
    rows, coords = train_grads.shape
    queries = query_cache.shape[1]
    own_tiles = rows // TILE
    batches = GROUPS // BATCH
    steps = (GROUPS // 2 + ring // 2) * PIECES
    sent = steps - PIECES
    dma = pltpu.SemaphoreType.DMA
    return pl.pallas_call(
        functools.partial(kernel, ring, turns),
        out_shape=jax.ShapeDtypeStruct((queries // owners, turns, rows), F32),
        in_specs=[
            pl.BlockSpec(memory_space=pl.ANY),
            pl.BlockSpec(memory_space=pl.ANY),
            pl.BlockSpec(memory_space=pltpu.VMEM),
            pl.BlockSpec(memory_space=pltpu.VMEM),
            pl.BlockSpec(memory_space=pltpu.SMEM),
            pl.BlockSpec(memory_space=pltpu.SMEM),
        ],
        out_specs=pl.BlockSpec(memory_space=pltpu.VMEM),
        scratch_shapes=[
            pltpu.VMEM((queries, coords), BF16),
            pltpu.VMEM((2 * own_tiles, TILE, BLOCK), BF16),
            pltpu.VMEM((32, BLOCK), F32),
            pltpu.VMEM((32, BLOCK), F32),
            pltpu.VMEM((BLOCK, BLOCK), BF16),
            pltpu.VMEM((BLOCK, BLOCK), BF16),
            pltpu.VMEM((256, 256), BF16),
            pltpu.VMEM((2, GROUPS, PIECES, 16, LANES), BF16),
            pltpu.VMEM((GROUPS, PIECES, 16, LANES), BF16),
            pltpu.VMEM((2 * sent, turns, 16, LANES), BF16),
            pltpu.VMEM((2 * steps, turns, 16, LANES), BF16),
            pltpu.VMEM((256, BLOCK), BF16),
            pltpu.VMEM((256, BLOCK), BF16),
            pltpu.VMEM((256, TILE), F32),
            pltpu.VMEM((batches, 2 * own_tiles, 16, TILE), F32),
            pltpu.VMEM((batches, own_tiles, 16, TILE), F32),
            pltpu.VMEM((own_tiles, 16 * batches, TILE), F32),
            pltpu.VMEM((batches, owners, 2 * own_tiles, 16, TILE), BF16),
            pltpu.VMEM((batches, owners, 2 * own_tiles, 16, TILE), BF16),
            dma((1 + own_tiles,)),
            dma((GROUPS,)),
            dma((GROUPS,)),
            dma((rows // PARCEL,)),
            dma((rows // PARCEL,)),
            dma((2 * sent,)),
            dma((2 * sent,)),
            dma((batches, owners)),
            dma((batches, owners)),
            dma((batches,)),
            dma((batches,)),
        ],
        compiler_params=pltpu.CompilerParams(
            collective_id=0, has_side_effects=True, vmem_limit_bytes=56 * 1024 * 1024
        ),
    )(train_grads, query_cache, left_inverse, right_inverse, module_of, owner)


def solution(mesh):
    placed = (P("example", "param"), P("example", None, "param"), P(), P(), P(), P())
    return jax.shard_map(
        body, mesh=mesh, in_specs=placed, out_specs=P("param", None, "example"), check_vma=False
    )
```

time: 145 us -> 109 us (0.75)
  Pallas kernels: 144 us -> 107 us
    pallas_call x1, Pallas kernels: 144 us -> 107 us  [body(): pl.pallas_call(functools.partial(kernel, ring, turns), out_shape=jax.Shap...]
where the time goes in v2:
time: 109 us
  Pallas kernels  107 us (98%)
  local copies, waits for them, and re-layouts  1.62 us (1%)
    pallas_call x1, Pallas kernels, body(): pl.pallas_call(functools.partial(kernel, ring, turns), out_shape=jax.Shap...  107 us

profile of v2, /device:TPU:1, one launch (start us, length us, event | category | flops | bytes accessed | tf_op | source)
XLA Modules:
  0.0 108.8 jit_solution(17939305299996893604)
XLA Ops:
  0.0 107.2 %shard_map.64 = f32[16,4,768]{2,1,0:T(4,128)} custom-call(bf16[768,2048]{1,0:T(8,128)(2,1)} %train_hbm.1, bf16[1,256,2048]{2,1,0:T(8,128)(2,1)} %query_hbm.1, f32[32,32,32]{2,1,0:T(8,128)} %left_ref.1, f32[32,32,32]{2,1,0:T(8,128)} %right_ref.1, s32[32]{0:T(128)} %module_ref.1, s32[4]{0:T(128)} %owner_ref.1), custom_call_target="tpu_custom_call" | custom-call | tf_op jit(solution)/shard_map/pallas_call | solution.py:418
  107.2 1.6 %copy.8 = f32[16,4,768]{2,1,0:T(4,128)} copy(f32[16,4,768]{2,1,0:T(4,128)} %shard_map.64) | data formatting | bytes 393216

commit v3 on v2

--- a/solution.py
+++ b/solution.py
@@ -37,6 +37,7 @@
     kron_high,
     kron_low,
     swapper,
+    regroup,
     mine,
     other,
     landed,
@@ -44,6 +45,7 @@
     gathered,
     sorted_rows,
     product,
+    paired,
     summed,
     crossed,
     ordered,
@@ -56,6 +58,8 @@
     train_recv,
     ring_send,
     ring_recv,
+    pair_send,
+    pair_recv,
     sum_send,
     sum_recv,
     cross_send,
@@ -64,6 +68,10 @@
     owners = lax.axis_size("param")
     param = lax.axis_index("param")
     example = lax.axis_index("example")
+    chips = owners // 2
+    chip = lax.div(param, 2)
+    core = lax.rem(param, 2)
+    sibling = chip * 2 + 1 - core
     plane = lax.div(example, 2)
     side = lax.rem(example, 2)
     partner = plane * 2 + 1 - side
@@ -75,7 +83,6 @@
     sent = steps - PIECES
     batches = GROUPS // BATCH
     own_tiles = train_hbm.shape[0] // TILE
-    tiles = 2 * own_tiles
 
     barrier = pltpu.get_barrier_semaphore()
     for place in (partner, following, previous):
@@ -83,12 +90,14 @@
             barrier, inc=1, device_id={"example": place}, device_id_type=MESH
         )
 
-    @pl.loop(1, owners)
+    pl.semaphore_signal(barrier, inc=1, device_id={"param": sibling}, device_id_type=MESH)
+
+    @pl.loop(1, chips)
     def _(hop):
         pl.semaphore_signal(
             barrier,
             inc=1,
-            device_id={"param": lax.rem(param + hop, owners)},
+            device_id={"param": lax.rem(chip + hop, chips) * 2 + core},
             device_id_type=MESH,
         )
 
@@ -124,13 +133,30 @@
     swapper[...] = (lax.bitwise_and(col, 15) * 16 + lax.shift_right_logical(col, 4) == row).astype(
         F32
     ).astype(BF16)
+    group_row = lax.bitwise_and(col, 15)
+    regroup[...] = (
+        lax.bitwise_and(group_row, 1) * (chips * 16)
+        + lax.shift_right_logical(group_row, 1) * 16
+        + lax.shift_right_logical(col, 4)
+        == row
+    ).astype(F32).astype(BF16)
+
+    def swap(order):
+        return pltpu.make_async_remote_copy(
+            src_ref=mine.at[1 - side, order],
+            dst_ref=other.at[order],
+            send_sem=swap_send.at[order],
+            recv_sem=swap_recv.at[order],
+            device_id={"example": partner},
+            device_id_type=MESH,
+        )
 
     factor = 1.0 / math.sqrt(2 * BLOCK * owners)
     col = lax.broadcasted_iota(jnp.int32, (32, BLOCK), 1)
     row = lax.broadcasted_iota(jnp.int32, (32, BLOCK), 0)
     pick_outer = (lax.shift_right_logical(col, 5) == row).astype(F32)
     pick_inner = (lax.bitwise_and(col, 31) == row).astype(F32)
-    for block in range(2):
+    for block, first in ((1 - side, True), (side, False)):
         module = module_ref[param * 2 + block]
         spread_left[...] = lax.dot_general(
             left_ref[module] * factor,
@@ -156,12 +182,12 @@
             kron_high[at, :] = high
             kron_low[at, :] = low
 
-        if block == 0:
-            pl.semaphore_wait(barrier, owners + 2)
+        if first:
+            pl.semaphore_wait(barrier, chips + 3)
             give_train(0).start()
             load_query.wait()
         source = jnp.dot(
-            swapper[...], query[:, block * BLOCK : (block + 1) * BLOCK], preferred_element_type=F32
+            swapper[...], query[:, pl.ds(pl.multiple_of(block * BLOCK, BLOCK), BLOCK)], preferred_element_type=F32
         ).astype(BF16)
         for k in range(BLOCK // TILE):
             cut = slice(k * TILE, (k + 1) * TILE)
@@ -173,25 +199,16 @@
                 mine[block, :, k * (TILE // LANES) + part] = mixed[
                     :, part * LANES : (part + 1) * LANES
                 ].reshape(GROUPS, 16, LANES)
-
-    def swap(order):
-        return pltpu.make_async_remote_copy(
-            src_ref=mine.at[1 - side, order],
-            dst_ref=other.at[order],
-            send_sem=swap_send.at[order],
-            recv_sem=swap_recv.at[order],
-            device_id={"example": partner},
-            device_id_type=MESH,
-        )
-
-    @pl.loop(0, GROUPS // 2)
-    def _(j):
-        swap(j).start()
-        swap(GROUPS - 1 - j).start()
-
-    @pl.loop(1, parcels)
-    def _(i):
-        give_train(i).start()
+        if first:
+
+            @pl.loop(0, GROUPS // 2)
+            def _(j):
+                swap(j).start()
+                swap(GROUPS - 1 - j).start()
+
+            @pl.loop(1, parcels)
+            def _(i):
+                give_train(i).start()
 
     roots = [lax.div(owner_ref[t], 2) for t in range(turns)]
     sides = [lax.rem(owner_ref[t], 2) for t in range(turns)]
@@ -224,7 +241,7 @@
             here = mine[side, order, k]
             there = other[order, k]
             if not first:
-                ring_copy(way, s - PIECES).wait_recv()
+                ring_copy(way, s - PIECES).wait()
             for t in range(turns):
                 value = jnp.where(sides[t] == side, here, there)
                 if not first:
@@ -254,30 +271,54 @@
                         k * LANES : (k + 1) * LANES,
                     ] = passed[base + k, t]
         sorted_rows[...] = jnp.dot(
-            swapper[...], gathered[...], preferred_element_type=F32
+            regroup[...], gathered[...], preferred_element_type=F32
         ).astype(BF16)
 
-    def multiply(b, j):
-        product[...] = lax.dot_general(
-            sorted_rows[...], train[j], ACROSS, preferred_element_type=F32
-        )
-        outgoing[b, :, j] = product[...].astype(BF16).reshape(owners, 16, TILE)
-        summed[b, j] = product[pl.ds(pl.multiple_of(param * 16, 16), 16), :]
-
-    def sum_copy(b, hop):
+    def pair_copy(b, part):
+        tiles_of = pl.ds(part * own_tiles, own_tiles)
         return pltpu.make_async_remote_copy(
-            src_ref=outgoing.at[b, lax.rem(param + hop, owners)],
-            dst_ref=incoming.at[b, hop],
-            send_sem=sum_send.at[b, hop],
-            recv_sem=sum_recv.at[b, hop],
-            device_id={"param": lax.rem(param + hop, owners)},
-            device_id_type=MESH,
-        )
-
-    def give(b):
-        @pl.loop(1, owners)
+            src_ref=product.at[b, 1 - core, tiles_of],
+            dst_ref=paired.at[b, tiles_of],
+            send_sem=pair_send.at[b, part],
+            recv_sem=pair_recv.at[b, part],
+            device_id={"param": sibling},
+            device_id_type=MESH,
+        )
+
+    def multiply(b, part):
+        @pl.loop(part * own_tiles, (part + 1) * own_tiles)
+        def _(j):
+            product[b, :, j] = lax.dot_general(
+                sorted_rows[...], train[j], ACROSS, preferred_element_type=F32
+            ).reshape(2, chips * 16, TILE)
+
+        pair_copy(b, part).start()
+
+    def sum_copy(b, part, hop):
+        tiles_of = pl.ds(part * own_tiles, own_tiles)
+        place = lax.rem(chip + hop, chips)
+        return pltpu.make_async_remote_copy(
+            src_ref=outgoing.at[b, place, tiles_of],
+            dst_ref=incoming.at[b, hop, tiles_of],
+            send_sem=sum_send.at[b, part, hop],
+            recv_sem=sum_recv.at[b, part, hop],
+            device_id={"param": place * 2 + core},
+            device_id_type=MESH,
+        )
+
+    def give(b, part):
+        pair_copy(b, part).wait_recv()
+
+        @pl.loop(part * own_tiles, (part + 1) * own_tiles)
+        def _(j):
+            both = product[b, core, j] + paired[b, j]
+            paired[b, j] = both
+            outgoing[b, :, j] = both.astype(BF16).reshape(chips, 16, TILE)
+            summed[b, j] = paired[b, j, pl.ds(pl.multiple_of(chip * 16, 16), 16), :]
+
+        @pl.loop(1, chips)
         def _(hop):
-            sum_copy(b, hop).start()
+            sum_copy(b, part, hop).start()
 
     def cross(b):
         return pltpu.make_async_remote_copy(
@@ -289,13 +330,21 @@
             device_id_type=MESH,
         )
 
-    def finish(b):
-        @pl.loop(1, owners)
+    def finish(b, part):
+        tiles_of = pl.ds(part * own_tiles, own_tiles)
+
+        @pl.loop(1, chips)
         def _(hop):
-            sum_copy(b, hop).wait_recv()
-            summed[b] += incoming[b, hop].astype(F32)
-
-        cross(b).start()
+            sum_copy(b, part, hop).wait_recv()
+            summed[b, tiles_of] += incoming[b, hop, tiles_of].astype(F32)
+
+        if part == 1:
+            cross(b).start()
+
+    def settle(b):
+        cross(b).wait_recv()
+        for j in range(own_tiles):
+            ordered[j, b * 16 : (b + 1) * 16, :] = summed[b, j] + crossed[b, j]
 
     start = (reach + 2) * PIECES
 
@@ -324,9 +373,7 @@
 
         @pl.when(jnp.logical_and(turn_of_batch, k == 1))
         def _():
-            @pl.loop(0, own_tiles)
-            def _(j):
-                multiply(b, j)
+            multiply(b, 0)
 
         @pl.when(jnp.logical_and(turn_of_batch, k == 2))
         def _():
@@ -336,34 +383,53 @@
                 def _(i):
                     give_train(i).wait_recv()
 
-            @pl.loop(own_tiles, tiles)
-            def _(j):
-                multiply(b, j)
-
-        @pl.when(jnp.logical_and(turn_of_batch, k == PIECES - 1))
-        def _():
-            give(b)
+            multiply(b, 1)
+
+        @pl.when(jnp.logical_and(turn_of_batch, k == 3))
+        def _():
+            give(b, 0)
+
+        @pl.when(jnp.logical_and(jnp.logical_not(turn_of_batch), k == 0))
+        def _():
+            give(b, 1)
+
+        @pl.when(jnp.logical_and(lap == 3, k == 2))
+        def _():
+            finish(0, 0)
+
+        @pl.when(jnp.logical_and(lap == 3, k == 3))
+        def _():
+            finish(0, 1)
 
     @pl.loop(sent, steps)
     def _(s):
         advance(s, False, True)
 
+        @pl.when(s == sent)
+        def _():
+            give(batches - 2, 1)
+
+        @pl.when(s == steps - 2)
+        def _():
+            finish(1, 0)
+
+        @pl.when(s == steps - 1)
+        def _():
+            finish(1, 1)
+
     gather(batches - 1)
-
-    @pl.loop(0, tiles)
-    def _(j):
-        multiply(batches - 1, j)
-
-    give(batches - 1)
-
-    @pl.loop(0, batches)
-    def _(b):
-        finish(b)
-
-    @pl.loop(0, sent)
-    def _(s):
-        ring_copy(0, s).wait_send()
-        ring_copy(1, s).wait_send()
+    multiply(batches - 1, 1)
+    multiply(batches - 1, 0)
+    give(batches - 1, 1)
+    give(batches - 1, 0)
+    for b in range(2, batches - 1):
+        finish(b, 1)
+        finish(b, 0)
+    for b in range(batches - 2):
+        settle(b)
+    finish(batches - 1, 1)
+    settle(batches - 2)
+    finish(batches - 1, 0)
 
     @pl.loop(0, GROUPS)
     def _(order):
@@ -373,16 +439,21 @@
     def _(i):
         give_train(i).wait_send()
 
+    for part in range(2):
+
+        @pl.loop(0, batches)
+        def _(b):
+            pair_copy(b, part).wait_send()
+
+            @pl.loop(1, chips)
+            def _(hop):
+                sum_copy(b, part, hop).wait_send()
+
+    settle(batches - 1)
+
     @pl.loop(0, batches)
     def _(b):
-        @pl.loop(1, owners)
-        def _(hop):
-            sum_copy(b, hop).wait_send()
-
-    for b in range(batches):
-        cross(b).wait()
-        for j in range(own_tiles):
-            ordered[j, b * 16 : (b + 1) * 16, :] = summed[b, j] + crossed[b, j]
+        cross(b).wait_send()
 
     for t in range(turns):
 
@@ -435,18 +506,20 @@
             pltpu.VMEM((BLOCK, BLOCK), BF16),
             pltpu.VMEM((BLOCK, BLOCK), BF16),
             pltpu.VMEM((256, 256), BF16),
+            pltpu.VMEM((256, 256), BF16),
             pltpu.VMEM((2, GROUPS, PIECES, 16, LANES), BF16),
             pltpu.VMEM((GROUPS, PIECES, 16, LANES), BF16),
             pltpu.VMEM((2 * sent, turns, 16, LANES), BF16),
             pltpu.VMEM((2 * steps, turns, 16, LANES), BF16),
             pltpu.VMEM((256, BLOCK), BF16),
             pltpu.VMEM((256, BLOCK), BF16),
-            pltpu.VMEM((256, TILE), F32),
+            pltpu.VMEM((batches, 2, 2 * own_tiles, 8 * owners, TILE), F32),
+            pltpu.VMEM((batches, 2 * own_tiles, 8 * owners, TILE), F32),
             pltpu.VMEM((batches, 2 * own_tiles, 16, TILE), F32),
             pltpu.VMEM((batches, own_tiles, 16, TILE), F32),
             pltpu.VMEM((own_tiles, 16 * batches, TILE), F32),
-            pltpu.VMEM((batches, owners, 2 * own_tiles, 16, TILE), BF16),
-            pltpu.VMEM((batches, owners, 2 * own_tiles, 16, TILE), BF16),
+            pltpu.VMEM((batches, owners // 2, 2 * own_tiles, 16, TILE), BF16),
+            pltpu.VMEM((batches, owners // 2, 2 * own_tiles, 16, TILE), BF16),
             dma((1 + own_tiles,)),
             dma((GROUPS,)),
             dma((GROUPS,)),
@@ -454,8 +527,10 @@
             dma((rows // PARCEL,)),
             dma((2 * sent,)),
             dma((2 * sent,)),
-            dma((batches, owners)),
-            dma((batches, owners)),
+            dma((batches, 2)),
+            dma((batches, 2)),
+            dma((batches, 2, owners // 2)),
+            dma((batches, 2, owners // 2)),
             dma((batches,)),
             dma((batches,)),
         ],

time: 109 us -> 101 us (0.927)
  Pallas kernels: 107 us -> 98.9 us
    pallas_call x1, Pallas kernels: 107 us -> 98.9 us  [body(): pl.pallas_call(functools.partial(kernel, ring, turns), out_shape=jax.Shap...]
where the time goes in v3:
time: 101 us
  Pallas kernels  98.9 us (98%)
  local copies, waits for them, and re-layouts  1.62 us (2%)
    pallas_call x1, Pallas kernels, body(): pl.pallas_call(functools.partial(kernel, ring, turns), out_shape=jax.Shap...  98.9 us

profile of v3, /device:TPU:1, one launch (start us, length us, event | category | flops | bytes accessed | tf_op | source)
XLA Modules:
  0.0 100.5 jit_solution(1831717081001554133)
XLA Ops:
  0.0 98.9 %shard_map.64 = f32[16,4,768]{2,1,0:T(4,128)} custom-call(bf16[768,2048]{1,0:T(8,128)(2,1)} %train_hbm.1, bf16[1,256,2048]{2,1,0:T(8,128)(2,1)} %query_hbm.1, f32[32,32,32]{2,1,0:T(8,128)} %left_ref.1, f32[32,32,32]{2,1,0:T(8,128)} %right_ref.1, s32[32]{0:T(128)} %module_ref.1, s32[4]{0:T(128)} %owner_ref.1), custom_call_target="tpu_custom_call" | custom-call | tf_op jit(solution)/shard_map/pallas_call | solution.py:489
  98.9 1.6 %copy.8 = f32[16,4,768]{2,1,0:T(4,128)} copy(f32[16,4,768]{2,1,0:T(4,128)} %shard_map.64) | data formatting | bytes 393216

commit v4 on v3

--- a/solution.py
+++ b/solution.py
@@ -14,7 +14,7 @@
 GROUPS = 16
 BATCH = 4
 TILE = 256
-PARCEL = 128
+PARCEL = 64
 MESH = pl.DeviceIdType.MESH
 BF16, F32 = jnp.bfloat16, jnp.float32
 ACROSS = (((1,), (1,)), ((), ()))
@@ -270,6 +270,8 @@
                         (u * turns + t) * 16 : (u * turns + t + 1) * 16,
                         k * LANES : (k + 1) * LANES,
                     ] = passed[base + k, t]
+
+    def sort_rows():
         sorted_rows[...] = jnp.dot(
             regroup[...], gathered[...], preferred_element_type=F32
         ).astype(BF16)
@@ -285,14 +287,12 @@
             device_id_type=MESH,
         )
 
-    def multiply(b, part):
-        @pl.loop(part * own_tiles, (part + 1) * own_tiles)
-        def _(j):
-            product[b, :, j] = lax.dot_general(
-                sorted_rows[...], train[j], ACROSS, preferred_element_type=F32
-            ).reshape(2, chips * 16, TILE)
-
-        pair_copy(b, part).start()
+    def multiply(b, j):
+        product[b, :, j] = lax.dot_general(
+            sorted_rows[...], train[j], ACROSS, preferred_element_type=F32
+        ).reshape(2, chips * 16, TILE)
+        if j % own_tiles == own_tiles - 1:
+            pair_copy(b, j // own_tiles).start()
 
     def sum_copy(b, part, hop):
         tiles_of = pl.ds(part * own_tiles, own_tiles)
@@ -359,68 +359,76 @@
     for copy in load_train:
         copy.wait()
 
+    def arrived(b, j):
+        @pl.when(b == 0)
+        def _():
+            @pl.loop((j - own_tiles) * (TILE // PARCEL), (j - own_tiles + 1) * (TILE // PARCEL))
+            def _(i):
+                give_train(i).wait_recv()
+
+    def work(s):
+        b = lax.div(s - start, 2 * PIECES)
+        k = lax.rem(s - start, 2 * PIECES)
+
+        @pl.when(k == 0)
+        def _():
+            gather(b)
+
+        @pl.when(k == 1)
+        def _():
+            sort_rows()
+            multiply(b, 0)
+
+        @pl.when(k == 2)
+        def _():
+            multiply(b, 1)
+            multiply(b, 2)
+
+        late = jnp.where(b == 0, 2, 0)
+
+        @pl.when(k == 3 + late)
+        def _():
+            arrived(b, 3)
+            multiply(b, 3)
+
+        @pl.when(k == 4 + late)
+        def _():
+            arrived(b, 4)
+            multiply(b, 4)
+            arrived(b, 5)
+            multiply(b, 5)
+
+        @pl.when(k == 5 - late)
+        def _():
+            give(b, 0)
+
+        @pl.when(k == jnp.where(b == 0, 7, 6))
+        def _():
+            give(b, 1)
+
+        @pl.when(jnp.logical_and(k == 7, b > 0))
+        def _():
+            finish(b - 1, 1)
+            finish(b - 1, 0)
+
     @pl.loop(start, sent)
     def _(s):
         advance(s, False, False)
-        lap = lax.div(s - start, PIECES)
-        k = lax.rem(s, PIECES)
-        b = lax.div(lap, 2)
-        turn_of_batch = lax.rem(lap, 2) == 0
-
-        @pl.when(jnp.logical_and(turn_of_batch, k == 0))
-        def _():
-            gather(b)
-
-        @pl.when(jnp.logical_and(turn_of_batch, k == 1))
-        def _():
-            multiply(b, 0)
-
-        @pl.when(jnp.logical_and(turn_of_batch, k == 2))
-        def _():
-            @pl.when(b == 0)
-            def _():
-                @pl.loop(0, parcels)
-                def _(i):
-                    give_train(i).wait_recv()
-
-            multiply(b, 1)
-
-        @pl.when(jnp.logical_and(turn_of_batch, k == 3))
-        def _():
-            give(b, 0)
-
-        @pl.when(jnp.logical_and(jnp.logical_not(turn_of_batch), k == 0))
-        def _():
-            give(b, 1)
-
-        @pl.when(jnp.logical_and(lap == 3, k == 2))
-        def _():
-            finish(0, 0)
-
-        @pl.when(jnp.logical_and(lap == 3, k == 3))
-        def _():
-            finish(0, 1)
+        work(s)
 
     @pl.loop(sent, steps)
     def _(s):
         advance(s, False, True)
-
-        @pl.when(s == sent)
-        def _():
-            give(batches - 2, 1)
-
-        @pl.when(s == steps - 2)
-        def _():
-            finish(1, 0)
-
-        @pl.when(s == steps - 1)
-        def _():
-            finish(1, 1)
+        work(s)
 
     gather(batches - 1)
-    multiply(batches - 1, 1)
+    sort_rows()
+    for j in range(own_tiles, 2 * own_tiles):
+        multiply(batches - 1, j)
     multiply(batches - 1, 0)
     give(batches - 1, 1)
+    for j in range(1, own_tiles):
+        multiply(batches - 1, j)
     give(batches - 1, 0)
     for b in range(2, batches - 1):
         finish(b, 1)

time: 101 us -> 96.6 us (0.956)
  Pallas kernels: 98.9 us -> 94.8 us
    pallas_call x1, Pallas kernels: 98.9 us -> 94.8 us  [body(): pl.pallas_call(functools.partial(kernel, ring, turns), out_shape=jax.Shap...]
where the time goes in v4:
time: 96.6 us; the launch traced here: 96.4 us
  Pallas kernels  94.8 us (98%)
  local copies, waits for them, and re-layouts  1.62 us (2%)
    pallas_call x1, Pallas kernels, body(): pl.pallas_call(functools.partial(kernel, ring, turns), out_shape=jax.Shap...  94.8 us

profile of v4, /device:TPU:1, one launch (start us, length us, event | category | flops | bytes accessed | tf_op | source)
XLA Modules:
  0.0 96.4 jit_solution(17120311321682547469)
XLA Ops:
  0.0 94.8 %shard_map.64 = f32[16,4,768]{2,1,0:T(4,128)} custom-call(bf16[768,2048]{1,0:T(8,128)(2,1)} %train_hbm.1, bf16[1,256,2048]{2,1,0:T(8,128)(2,1)} %query_hbm.1, f32[32,32,32]{2,1,0:T(8,128)} %left_ref.1, f32[32,32,32]{2,1,0:T(8,128)} %right_ref.1, s32[32]{0:T(128)} %module_ref.1, s32[4]{0:T(128)} %owner_ref.1), custom_call_target="tpu_custom_call" | custom-call | tf_op jit(solution)/shard_map/pallas_call | solution.py:497
  94.8 1.6 %copy.8 = f32[16,4,768]{2,1,0:T(4,128)} copy(f32[16,4,768]{2,1,0:T(4,128)} %shard_map.64) | data formatting | bytes 393216

commit v5 on v4

--- a/solution.py
+++ b/solution.py
@@ -25,11 +25,13 @@
     turns,
     train_hbm,
     query_hbm,
-    left_ref,
-    right_ref,
+    left_hbm,
+    right_hbm,
     module_ref,
     owner_ref,
     out_ref,
+    left_ref,
+    right_ref,
     query,
     train,
     spread_left,
@@ -103,6 +105,12 @@
 
     load_query = pltpu.make_async_copy(query_hbm.at[0], query, load_sem.at[0])
     load_query.start()
+    load_sides = [
+        pltpu.make_async_copy(left_hbm, left_ref, load_sem.at[1 + own_tiles]),
+        pltpu.make_async_copy(right_hbm, right_ref, load_sem.at[2 + own_tiles]),
+    ]
+    for copy in load_sides:
+        copy.start()
     here_lanes = pl.ds(pl.multiple_of(side * BLOCK, BLOCK), BLOCK)
     there_lanes = pl.ds(pl.multiple_of((1 - side) * BLOCK, BLOCK), BLOCK)
     load_train = [
@@ -156,6 +164,8 @@
     row = lax.broadcasted_iota(jnp.int32, (32, BLOCK), 0)
     pick_outer = (lax.shift_right_logical(col, 5) == row).astype(F32)
     pick_inner = (lax.bitwise_and(col, 31) == row).astype(F32)
+    for copy in load_sides:
+        copy.wait()
     for block, first in ((1 - side, True), (side, False)):
         module = module_ref[param * 2 + block]
         spread_left[...] = lax.dot_general(
@@ -465,7 +475,7 @@
 
     for t in range(turns):
 
-        @pl.loop(0, GROUPS)
+        @pl.loop(0, GROUPS, unroll=4)
         def _(i):
             a = jnp.where(near[t] == 0, i, GROUPS - 1 - i)
             v = jnp.where(
@@ -500,13 +510,15 @@
         in_specs=[
             pl.BlockSpec(memory_space=pl.ANY),
             pl.BlockSpec(memory_space=pl.ANY),
-            pl.BlockSpec(memory_space=pltpu.VMEM),
-            pl.BlockSpec(memory_space=pltpu.VMEM),
+            pl.BlockSpec(memory_space=pl.ANY),
+            pl.BlockSpec(memory_space=pl.ANY),
             pl.BlockSpec(memory_space=pltpu.SMEM),
             pl.BlockSpec(memory_space=pltpu.SMEM),
         ],
         out_specs=pl.BlockSpec(memory_space=pltpu.VMEM),
         scratch_shapes=[
+            pltpu.VMEM(left_inverse.shape, F32),
+            pltpu.VMEM(right_inverse.shape, F32),
             pltpu.VMEM((queries, coords), BF16),
             pltpu.VMEM((2 * own_tiles, TILE, BLOCK), BF16),
             pltpu.VMEM((32, BLOCK), F32),
@@ -528,7 +540,7 @@
             pltpu.VMEM((own_tiles, 16 * batches, TILE), F32),
             pltpu.VMEM((batches, owners // 2, 2 * own_tiles, 16, TILE), BF16),
             pltpu.VMEM((batches, owners // 2, 2 * own_tiles, 16, TILE), BF16),
-            dma((1 + own_tiles,)),
+            dma((3 + own_tiles,)),
             dma((GROUPS,)),
             dma((GROUPS,)),
             dma((rows // PARCEL,)),

time: 96.6 us -> 95.8 us (level)
  no operation moved by 1% of the time
where the time goes in v5:
time: 95.8 us; the launch traced here: 95.7 us
  Pallas kernels  94 us (98%)
  local copies, waits for them, and re-layouts  1.62 us (2%)
    pallas_call x1, Pallas kernels, body(): pl.pallas_call(functools.partial(kernel, ring, turns), out_shape=jax.Shap...  94 us

profile of v5, /device:TPU:1, one launch (start us, length us, event | category | flops | bytes accessed | tf_op | source)
XLA Modules:
  0.0 95.7 jit_solution(15495764871330709768)
XLA Ops:
  0.0 94.0 %shard_map.64 = f32[16,4,768]{2,1,0:T(4,128)} custom-call(bf16[768,2048]{1,0:T(8,128)(2,1)} %train_hbm.1, bf16[1,256,2048]{2,1,0:T(8,128)(2,1)} %query_hbm.1, f32[32,32,32]{2,1,0:T(8,128)} %left_hbm.1, f32[32,32,32]{2,1,0:T(8,128)} %right_hbm.1, s32[32]{0:T(128)} %module_ref.1, s32[4]{0:T(128)} %owner_ref.1), custom_call_target="tpu_custom_call" | custom-call | tf_op jit(solution)/shard_map/pallas_call | solution.py:507
  94.1 1.6 %copy.8 = f32[16,4,768]{2,1,0:T(4,128)} copy(f32[16,4,768]{2,1,0:T(4,128)} %shard_map.64) | data formatting | bytes 393216
